TPU v7x, 32 devices: a whole 2x2x4 slice. The times are simulated.
32 devices in a mesh: snap: 1, dom: 16 (over z, y, x), rep: 2 (over core).
Axes of the slice: x: 2, y: 2, z: 4, core: 2. Of those that a mesh axis runs over, the one named last changes fastest.
Arguments:
- features: bfloat16 [1, 4096, 512], P('snap', 'dom'), may hold values from -6 to 6
- tiles: bfloat16 [1, 32, 6, 128, 128], P('snap', ('dom', 'rep')), may hold values from 0.099609375 to 1
- tile_cols: int32 [1, 32, 6], P('snap', ('dom', 'rep')), may hold values from 0 to 5, as said below
- tile_count: int32 [1, 32], P('snap', ('dom', 'rep')), may hold values from 1 to 6, as said below
- boundary_rows: int32 [1, 16, 16, 32], P('snap', 'dom'), may hold values from 0 to 255
- boundary_count: int32 [1, 16, 16], P('snap', 'dom'), may hold values from 16 to 32, as said below
- cotangent: bfloat16 [1, 4096, 512], P('snap', ('dom', 'rep')), may hold values from -6 to 6
- w_init: float32 [512, 512], P(None, 'dom'), may hold values from -0.25 to 0.25
- update_map: bfloat16 [512, 512], replicated, may hold values from -0.25 to 0.25
- reset_map: bfloat16 [512, 512], replicated, may hold values from -0.25 to 0.25
- cand_input: bfloat16 [512, 512], replicated, may hold values from -0.25 to 0.25
- cand_hidden: bfloat16 [512, 512], replicated, may hold values from -0.25 to 0.25
- update_bias: float32 [512, 512], P(None, 'dom'), may hold values from -6 to 6
- reset_bias: float32 [512, 512], P(None, 'dom'), may hold values from -6 to 6
- cand_bias: float32 [512, 512], P(None, 'dom'), may hold values from -6 to 6
Outputs:
- grad_features: bfloat16 [1, 4096, 512], P('snap', ('dom', 'rep'))
- grad_weights: float32 [1, 512, 512], P('snap', ('dom', 'rep'))
Inputs may be any that keep to these rules, and one draw needn't show every extreme that they name: `tile_cols`: the 6 column blocks of one row block are distinct. `tile_count`: every row block of a partition whose index is a multiple of 4 has 6 live slots. `boundary_count`: a source and destination pair whose indices sum to a multiple of 3 has all 32 slots live.
All inputs are finite; a program needn't handle non-finite values.
Results may differ from a plain program's by a relative error of at most 0.009.
Values may be sent and summed in bfloat16 or wider, within the bound.
A program may use at most 64 MiB of HBM per device.

v0:
```python
import jax
import jax.numpy as jnp
from jax import lax
from jax.sharding import PartitionSpec as P

BND = 32
TILE = 128
KMAX = 6


def shifted(block, axis, distance):
    devices = range(lax.axis_size(axis))
    route = [(i - distance, i) for i in devices if i - distance in devices]
    return lax.ppermute(block, axis, route)


def evolve_step(hidden_w, params):
    update_map, reset_map, cand_input, cand_hidden, update_bias, reset_bias, cand_bias = params
    state_bf = hidden_w.astype(jnp.bfloat16)
    update = jax.nn.sigmoid(
        jnp.dot(update_map, state_bf, preferred_element_type=jnp.float32) + update_bias
    )
    reset = jax.nn.sigmoid(
        jnp.dot(reset_map, state_bf, preferred_element_type=jnp.float32) + reset_bias
    )
    gated_state = (reset * hidden_w).astype(jnp.bfloat16)
    candidate = jnp.tanh(
        jnp.dot(cand_input, state_bf, preferred_element_type=jnp.float32)
        + jnp.dot(cand_hidden, gated_state, preferred_element_type=jnp.float32)
        + cand_bias
    )
    return (1.0 - update) * hidden_w + update * candidate


def pick_rows(source_rows, indices):
    return source_rows[indices]


def local(
    features,
    tiles,
    tile_cols,
    tile_count,
    boundary_rows,
    boundary_count,
    cotangent,
    w_init,
    update_map,
    reset_map,
    cand_input,
    cand_hidden,
    update_bias,
    reset_bias,
    cand_bias,
):
    per_owner = features.shape[0]
    node_rows = features.shape[1]
    width = features.shape[2]
    parts = lax.axis_size("dom")
    owner = lax.axis_index("snap")
    owners = lax.axis_size("snap")
    params = (update_map, reset_map, cand_input, cand_hidden, update_bias, reset_bias, cand_bias)
    slot_ids = jnp.arange(per_owner, dtype=jnp.int32)
    stored_init = jnp.zeros((per_owner,) + w_init.shape, jnp.float32)

    def handoff_turn(step_no, carried):
        current, stored = carried
        active = owner == step_no
        evolved = evolve_step(current, params)
        current = jnp.where(active, evolved, current)
        chosen = active & (slot_ids == 0)
        stored = jnp.where(chosen[:, None, None], evolved[None], stored)
        current = shifted(current, "snap", 1)
        return (current, stored)

    unused_state, stored = lax.fori_loop(0, owners, handoff_turn, (w_init, stored_init))
    weights = lax.all_gather(stored.astype(jnp.bfloat16), "dom", axis=2, tiled=True)
    brows = boundary_rows[:, 0]
    bcounts = boundary_count[:, 0]
    live_slots = jnp.arange(BND, dtype=jnp.int32)[None, None, :] < bcounts[:, :, None]
    outgoing = jax.vmap(pick_rows)(features, brows)
    outgoing = jnp.where(live_slots[..., None], outgoing, jnp.zeros((), jnp.bfloat16))
    halo_rows = lax.all_to_all(outgoing, "dom", split_axis=1, concat_axis=1, tiled=True)
    extended = jnp.concatenate([features, halo_rows.reshape(per_owner, parts * BND, width)], axis=1)
    col_blocks = extended.shape[1] // TILE
    extended = extended.reshape(per_owner, col_blocks, TILE, width)
    tile_live = jnp.arange(KMAX, dtype=jnp.int32)[None, None, :] < tile_count[..., None]
    adjacency = jnp.where(tile_live[..., None, None], tiles, jnp.zeros((), jnp.bfloat16))
    gathered = jax.vmap(pick_rows)(extended, tile_cols)
    summed = jnp.einsum(
        "srkij,srkjf->srif", adjacency, gathered, preferred_element_type=jnp.float32
    )
    degree = jnp.sum(adjacency, axis=(2, 4), dtype=jnp.float32)
    my_blocks = tiles.shape[1]
    aggregated = (
        (summed / degree[..., None])
        .astype(jnp.bfloat16)
        .reshape(per_owner, my_blocks * TILE, width)
    )
    preact = jnp.einsum("snf,sfg->sng", aggregated, weights, preferred_element_type=jnp.float32)
    sigma_pre = jax.nn.sigmoid(preact)
    grad_pre = (
        cotangent.astype(jnp.float32) * sigma_pre * (1.0 + preact * (1.0 - sigma_pre))
    ).astype(jnp.bfloat16)
    grad_rows = lax.psum_scatter(
        jnp.einsum("sni,snj->isj", aggregated, grad_pre, preferred_element_type=jnp.float32),
        ("dom", "rep"),
        scatter_dimension=0,
        tiled=True,
    )
    grad_weights = jnp.transpose(grad_rows, (1, 0, 2))
    grad_mixed = jnp.einsum("sng,sfg->snf", grad_pre, weights, preferred_element_type=jnp.float32)
    grad_summed = (
        grad_mixed.reshape(per_owner, my_blocks, TILE, width) / degree[..., None]
    ).astype(jnp.bfloat16)
    grad_blocks = jnp.einsum(
        "srkij,srif->srkjf", adjacency, grad_summed, preferred_element_type=jnp.float32
    )

    def add_blocks(columns, blocks_in):
        return jnp.zeros((col_blocks, TILE, width), jnp.float32).at[columns].add(blocks_in)

    grad_ext = jax.vmap(add_blocks)(tile_cols, grad_blocks).reshape(
        per_owner, col_blocks * TILE, width
    )
    grad_local = grad_ext[:, :node_rows]
    grad_halo = grad_ext[:, node_rows:].reshape(per_owner, parts, BND, width)
    returned = lax.all_to_all(grad_halo, "dom", split_axis=1, concat_axis=1, tiled=True)
    returned = jnp.where(live_slots[..., None], returned, jnp.zeros((), jnp.float32))

    def add_rows(grad_part, indices, incoming):
        return grad_part.at[indices.reshape(-1)].add(incoming.reshape(-1, width))

    grad_local = jax.vmap(add_rows)(grad_local, brows, returned)
    grad_features = lax.psum_scatter(grad_local, "rep", scatter_dimension=1, tiled=True).astype(
        jnp.bfloat16
    )
    return (grad_features, grad_weights)


def solution(mesh):
    in_specs = (
        P("snap", "dom", None),
        P("snap", ("dom", "rep"), None, None, None),
        P("snap", ("dom", "rep"), None),
        P("snap", ("dom", "rep")),
        P("snap", "dom", None, None),
        P("snap", "dom", None),
        P("snap", ("dom", "rep"), None),
        P(None, "dom"),
        P(),
        P(),
        P(),
        P(),
        P(None, "dom"),
        P(None, "dom"),
        P(None, "dom"),
    )
    out_specs = (P("snap", ("dom", "rep"), None), P("snap", ("dom", "rep"), None))
    return jax.shard_map(local, mesh=mesh, in_specs=in_specs, out_specs=out_specs, check_vma=False)
```

profile of v0, /device:TPU:0, one launch (start us, length us, event | category | flops | bytes accessed | tf_op | source)
XLA Modules:
  0.0 230.2 jit_solution(13031282687127576058)
XLA Ops:
  8.0 0.0 copy-start
  8.0 0.8 iota_compare_fusion
  8.8 0.7 compare_select_fusion
  9.5 0.1 reshape.212
  9.6 4.3 %gather_fusion = bf16[512,512]{1,0:T(8,128)(2,1)S(1)} fusion(bf16[1,256,512]{2,1,0:T(8,128)(2,1)} %param.15, s32[512]{0:T(512)S(1)} %reshape.212), kind=kCustom, calls=%fused_computation | custom fusion | bytes 1052672 | tf_op jit(solution)/shard_map/vmap()/gather | solution.py:36
  13.9 0.0 copy-start.13
  13.9 0.0 copy-start.7
  13.9 0.0 copy-start.3
  13.9 0.0 copy-start.4
  13.9 0.0 copy-start.10
  13.9 0.9 broadcast_select_fusion.1
  14.9 0.0 copy-start.5
  14.9 0.0 copy-start.6
  14.9 0.0 copy-start.8
  14.9 0.0 copy-start.9
  14.9 8.5 %all-to-all-start = ((bf16[1,16,32,512]{3,2,0,1:T(8,128)(2,1)}), bf16[1,16,32,512]{3,2,0,1:T(8,128)(2,1)S(1)}, u32[]{:S(2)}, u32[]{:S(2)}) async-start(bf16[1,16,32,512]{3,2,0,1:T(8,128)(2,1)} %broadcast_select_fusion.1), calls=%async_computation | async-start | bytes 1048576 | tf_op jit(solution)/shard_map/all_to_all | solution.py:83
  24.0 0.0 copy-done.13
  24.0 0.0 copy-done.7
  24.1 0.2 convert_reduce_fusion
  24.2 0.0 copy-done
  24.3 0.0 copy-done.3
  24.3 0.0 copy-start.2
  24.3 0.2 fusion.39
  24.5 0.0 copy-done.4
  24.5 0.0 copy-done.10
  24.5 0.3 fusion.8
  24.8 0.0 copy-done.5
  24.8 0.0 copy-done.6
  24.9 0.0 copy-done.8
  24.9 0.0 copy-done.9
  24.9 0.5 fusion.16
  25.4 44.5 %all-gather = bf16[512,512]{0,1:T(8,128)(2,1)S(1)} all-gather(bf16[512,32]{0,1:T(8,128)(2,1)S(1)} %fusion.16), channel_id=2, replica_groups=mesh['snap'=1,'dom'=16,'rep'=2] {'dom'}, dimensions={1}, use_global_device_ids=true | all-gather | bytes 557056 | tf_op jit(solution)/shard_map/all_gather | solution.py:77
  69.9 0.0 all-to-all-done
  69.9 0.0 copy-done.2
  69.9 0.1 pad_maximum_fusion
  69.9 0.6 gather_fusion.1
  70.5 0.0 copy-start.12
  70.5 0.3 fusion.19
  70.9 0.3 fusion.46
  71.2 0.3 copy-done.12
  71.4 1.8 fusion.20
  73.2 0.2 broadcast.140
  73.4 2.9 %scatter_fusion = f32[6,128,512]{2,1,0:T(8,128)S(1)} fusion(f32[6,128,512]{2,1,0:T(8,128)S(1)} %broadcast.140, s32[6]{0:T(128)S(1)} %get-tuple-element.31, f32[6,128,512]{2,1,0:T(8,128)} %fusion.20), kind=kCustom, calls=%fused_computation.2 | custom fusion | flops 393216 | bytes 4718616 | tf_op jit(solution)/shard_map/vmap()/scatter-add | solution.py:121
  76.3 1.1 slice.21
  77.3 0.0 copy-start.11
  77.3 4.5 %all-to-all-start.1 = ((f32[1,16,32,512]{3,2,0,1:T(8,128)}), f32[1,16,32,512]{3,2,0,1:T(8,128)}, u32[]{:S(2)}, u32[]{:S(2)}) async-start(f32[1,16,32,512]{3,2,0,1:T(8,128)} %bitcast.23), calls=%async_computation.1 | async-start | bytes 2097152 | tf_op jit(solution)/shard_map/all_to_all | solution.py:128
  81.8 0.0 all-reduce.3.cloned.1.call-start
  81.9 0.0 copy-done.11
  81.9 0.1 reshape_squeeze.3
  82.0 1.3 convolution_bitcast_fusion
  83.2 2.0 copy.21
  85.2 0.0 all-reduce.3.cloned.1.call-update
  85.2 0.0 reduce-scatter.2.cloned.1.call-start
  85.3 14.3 %all-to-all-done.1 = f32[1,16,32,512]{3,2,0,1:T(8,128)} async-done(((f32[1,16,32,512]{3,2,0,1:T(8,128)}), f32[1,16,32,512]{3,2,0,1:T(8,128)}, u32[]{:S(2)}, u32[]{:S(2)}) %all-to-all-start.1) | async-done | bytes 1048608 | tf_op jit(solution)/shard_map/all_to_all | solution.py:128
  99.6 1.4 broadcast_select_fusion
  101.0 3.8 %scatter_fusion.1 = f32[256,512]{1,0:T(8,128)S(1)} fusion(f32[256,512]{1,0:T(8,128)S(1)} %slice_bitcast_fusion, s32[512]{0:T(512)S(1)} %bitcast.112, f32[512,512]{1,0:T(8,128)S(1)} %bitcast.108), kind=kCustom, calls=%fused_computation.3 | custom fusion | flops 262144 | bytes 3147776 | tf_op jit(solution)/shard_map/vmap()/scatter-add | solution.py:132
  104.8 0.0 copy-start.1
  104.8 0.8 copy-done.1
  105.6 0.0 reduce-scatter.2.cloned.1.call-update
  105.6 114.1 %all-reduce.3.cloned.1.call-done = f32[512,1,512]{2,1,0:T(1,128)} async-done(((f32[512,1,512]{2,1,0:T(1,128)}), f32[512,1,512]{2,1,0:T(1,128)}) %all-reduce.3.cloned.1.call-update) | async-done | bytes 1048592
  219.7 0.8 dynamic-slice_bitcast_fusion
  220.5 0.6 copy.22
  221.1 0.0 reduce-scatter.2.cloned.1.call-done
  221.1 1.6 convert_element_type.43
  (10 shorter events, 0.1 us)
Async XLA Ops:
  8.0 16.3 %copy-start = (bf16[512,512]{1,0:T(8,128)(2,1)S(1)}, bf16[512,512]{1,0:T(8,128)(2,1)}, u32[]{:S(2)}) copy-start(bf16[512,512]{1,0:T(8,128)(2,1)} %param.25) | copy-start | bytes 1572868
  13.9 10.1 %copy-start.13 = (s32[1,1,6]{2,1,0:T(1,128)S(1)}, s32[1,1,6]{2,1,0:T(1,128)}, u32[]{:S(2)}) copy-start(s32[1,1,6]{2,1,0:T(1,128)} %param.17) | copy-start | bytes 76
  13.9 10.2 %copy-start.7 = (bf16[1,1,6,128,128]{4,3,2,1,0:T(8,128)(2,1)S(1)}, bf16[1,1,6,128,128]{4,3,2,1,0:T(8,128)(2,1)}, u32[]{:S(2)}) copy-start(bf16[1,1,6,128,128]{4,3,2,1,0:T(8,128)(2,1)} %param.16) | copy-start | bytes 589828
  13.9 10.4 %copy-start.3 = (f32[512,32]{0,1:T(8,128)S(1)}, f32[512,32]{0,1:T(8,128)}, u32[]{:S(2)}) copy-start(f32[512,32]{0,1:T(8,128)} %param.22) | copy-start | bytes 196612
  13.9 10.6 %copy-start.4 = (bf16[512,512]{1,0:T(8,128)(2,1)S(1)}, bf16[512,512]{1,0:T(8,128)(2,1)}, u32[]{:S(2)}) copy-start(bf16[512,512]{1,0:T(8,128)(2,1)} %param.23) | copy-start | bytes 1572868
  13.9 10.6 %copy-start.10 = (f32[512,32]{0,1:T(8,128)S(1)}, f32[512,32]{0,1:T(8,128)}, u32[]{:S(2)}) copy-start(f32[512,32]{0,1:T(8,128)} %param.27) | copy-start | bytes 196612
  14.9 10.0 %copy-start.5 = (bf16[512,512]{1,0:T(8,128)(2,1)S(1)}, bf16[512,512]{1,0:T(8,128)(2,1)}, u32[]{:S(2)}) copy-start(bf16[512,512]{1,0:T(8,128)(2,1)} %param.26) | copy-start | bytes 1572868
  14.9 10.0 %copy-start.6 = (bf16[512,512]{1,0:T(8,128)(2,1)S(1)}, bf16[512,512]{1,0:T(8,128)(2,1)}, u32[]{:S(2)}) copy-start(bf16[512,512]{1,0:T(8,128)(2,1)} %param.24) | copy-start | bytes 1572868
  14.9 10.0 %copy-start.8 = (f32[512,32]{0,1:T(8,128)S(1)}, f32[512,32]{0,1:T(8,128)}, u32[]{:S(2)}) copy-start(f32[512,32]{0,1:T(8,128)} %param.29) | copy-start | bytes 196612
  14.9 10.0 %copy-start.9 = (f32[512,32]{0,1:T(8,128)S(1)}, f32[512,32]{0,1:T(8,128)}, u32[]{:S(2)}) copy-start(f32[512,32]{0,1:T(8,128)} %param.28) | copy-start | bytes 196612
  14.9 55.0 %all-to-all-start = ((bf16[1,16,32,512]{3,2,0,1:T(8,128)(2,1)}), bf16[1,16,32,512]{3,2,0,1:T(8,128)(2,1)S(1)}, u32[]{:S(2)}, u32[]{:S(2)}) async-start(bf16[1,16,32,512]{3,2,0,1:T(8,128)(2,1)} %broadcast_select_fusion.1), calls=%async_computation | async-start | bytes 1048576 | tf_op jit(solution)/shard_map/all_to_all | solution.py:83
  24.3 45.6 %copy-start.2 = (bf16[1,256,512]{2,1,0:T(8,128)(2,1)S(1)}, bf16[1,256,512]{2,1,0:T(8,128)(2,1)}, u32[]{:S(2)}) copy-start(bf16[1,256,512]{2,1,0:T(8,128)(2,1)} %param.15) | copy-start | bytes 786436
  70.5 0.9 copy-start.12
  77.3 4.5 %copy-start.11 = (s32[1,1,16,32]{3,2,1,0:T(8,128)S(1)}, s32[1,1,16,32]{3,2,1,0:T(8,128)}, u32[]{:S(2)}) copy-start(s32[1,1,16,32]{3,2,1,0:T(8,128)} %param.19) | copy-start | bytes 6148
  77.3 22.3 %all-to-all-start.1 = ((f32[1,16,32,512]{3,2,0,1:T(8,128)}), f32[1,16,32,512]{3,2,0,1:T(8,128)}, u32[]{:S(2)}, u32[]{:S(2)}) async-start(f32[1,16,32,512]{3,2,0,1:T(8,128)} %bitcast.23), calls=%async_computation.1 | async-start | bytes 2097152 | tf_op jit(solution)/shard_map/all_to_all | solution.py:128
  81.8 137.9 %all-reduce.3.cloned.1.call-start = ((), (), s32[]{:S(2)}) async-start(), calls=%async_computation.4 | async-start | bytes 2097152
  85.2 135.9 %reduce-scatter.2.cloned.1.call-start = ((), (), s32[]{:S(2)}) async-start(), calls=%async_computation.3 | async-start | bytes 786432 | tf_op jit(solution)/shard_map/reduce_scatter | solution.py:135
  104.8 0.8 copy-start.1
Sparse Core Ops, SparseCore 0:
  88.7 131.0 all-reduce.2
Sparse Core Ops, SparseCore 1:
  105.7 7.6 reduce-scatter.1
where the time goes:
time: 231 us; the launch traced here: 230 us
  waiting for transfers between devices  128 us (55%)
  blocking collectives  44.5 us (19%)
  between operations  16.4 us (7%)
  starting transfers between devices  13 us (6%)
  other arithmetic  12.4 us (5%)
  local copies, waits for them, and re-layouts  10.8 us (5%)
  matrix products  4.63 us (2%)
    unnamed x3, waiting for transfers between devices  114 us
    all_gather x1, blocking collectives, local(): lax.all_gather(stored.astype(jnp.bfloat16), 'dom', axis=2, tiled=True)  44.5 us
    all_to_all x1, waiting for transfers between devices, local(): lax.all_to_all(grad_halo, 'dom', split_axis=1, concat_axis=1, tiled=True)  14.3 us
    all_to_all x1, starting transfers between devices, local(): lax.all_to_all(outgoing, 'dom', split_axis=1, concat_axis=1, tiled=True)  8.46 us
    gather x4, local copies, waits for them, and re-layouts, pick_rows(): return source_rows[indices]  4.95 us
  transfers between devices with their start and end apart: 4, of which 2 were waited for; matrix products, arithmetic and copies ran while one was open for 5% of the time, Pallas kernels for 0%

commit v1 on v0

v1 whole, which is shorter than its diff:
```python
import functools

import jax
import jax.numpy as jnp
from jax import lax
from jax.experimental import pallas as pl
from jax.experimental.pallas import tpu as pltpu
from jax.sharding import PartitionSpec as P

TILE = 128
MESH = pl.DeviceIdType.MESH
F32 = jnp.float32
BF16 = jnp.bfloat16


def dot(a, b, dims):
    return lax.dot_general(a, b, (dims, ((), ())), preferred_element_type=F32)


NN = ((1,), (0,))
NT = ((1,), (1,))
TN = ((0,), (0,))


def gru_rows(state, um, rm, ci, ch, ub, rb, cb):
    state_bf = state.astype(BF16)
    update = jax.nn.sigmoid(dot(state_bf, um, NT) + ub)
    reset = jax.nn.sigmoid(dot(state_bf, rm, NT) + rb)
    gated = (reset * state).astype(BF16)
    candidate = jnp.tanh(dot(state_bf, ci, NT) + dot(gated, ch, NT) + cb)
    return (1.0 - update) * state + update * candidate


def kernel(
    n,
    feat,
    tiles,
    inv,
    live,
    rowsel,
    cot,
    state,
    um,
    rm,
    ci,
    ch,
    ub,
    rb,
    cb,
    out_x,
    out_w,
    adj,
    ext,
    halo_out,
    cot_all,
    wt_mine,
    wt,
    agg,
    gm_out,
    gm_in,
    ret_out,
    ret_in,
    gw_out,
    gw_in,
    gws_out,
    gws_in,
    fin_out,
    fin_in,
    pair_send,
    pair_recv,
    halo_send,
    halo_recv,
    w_send,
    w_recv,
    ret_send,
    ret_recv,
    gw_send,
    gw_recv,
):
    me = lax.axis_index("dom")
    r = lax.axis_index("rep")
    other = 1 - r
    nodes, width = feat.shape
    half = width // 2
    nb = rowsel.shape[1] // n
    wrows = wt_mine.shape[0]
    per_half = half // wrows
    ncb = adj.shape[1] // TILE
    wsplit = gws_out.shape[0]

    def cols(which):
        return pl.ds(pl.multiple_of(which * half, half), half)

    def at(i, size):
        return pl.ds(pl.multiple_of(i * size, size), size)

    mine_rows = at(r, TILE)
    mine_cols, other_cols = cols(r), cols(other)

    barrier = pltpu.get_barrier_semaphore()

    def greet(i, c):
        q = lax.rem(me + i, n)
        pl.semaphore_signal(barrier, inc=1, device_id={"dom": q, "rep": other}, device_id_type=MESH)

        @pl.when(i != 0)
        def _():
            pl.semaphore_signal(barrier, inc=1, device_id={"dom": q, "rep": r}, device_id_type=MESH)

        return c

    lax.fori_loop(0, n, greet, 0)

    for c in range(ncb):
        tile = tiles[inv[c]].astype(F32) * live[c]
        adj[mine_rows, c * TILE : (c + 1) * TILE] = tile.astype(BF16)
    cot_all[mine_rows, :] = cot[:, mine_cols]

    picks = (lax.broadcasted_iota(jnp.int32, (nodes, n * nb), 0) == rowsel[...]).astype(F32).astype(BF16)
    my_feat = feat[:, mine_cols]
    halo_out[...] = dot(picks, my_feat, TN).astype(BF16)

    pl.semaphore_wait(barrier, 2 * n - 1)

    def to_pair(slot, src, dst):
        copy = pltpu.make_async_remote_copy(
            src_ref=src,
            dst_ref=dst,
            send_sem=pair_send.at[slot],
            recv_sem=pair_recv.at[slot],
            device_id={"dom": me, "rep": other},
            device_id_type=MESH,
        )
        copy.start()
        return copy

    def spread_copy(d, out_ref, in_ref, size, send_sem, recv_sem):
        q = lax.rem(me + d, n)
        return pltpu.make_async_remote_copy(
            src_ref=out_ref.at[at(q, size)],
            dst_ref=in_ref.at[at(me, size)],
            send_sem=send_sem.at[d],
            recv_sem=recv_sem.at[d],
            device_id={"dom": q, "rep": r},
            device_id_type=MESH,
        )

    def spread_start(*how):
        def go(d, c):
            spread_copy(d, *how).start()
            return c

        lax.fori_loop(1, n, go, 0)

    def spread_wait(out_ref, in_ref, size, send_sem, recv_sem):
        def go(d, c):
            src = lax.rem(me + n - d, n)
            pltpu.make_async_remote_copy(
                src_ref=out_ref.at[at(src, size)],
                dst_ref=in_ref.at[at(src, size)],
                send_sem=send_sem.at[d],
                recv_sem=recv_sem.at[d],
                device_id={"dom": src, "rep": r},
                device_id_type=MESH,
            ).wait_recv()
            return c

        lax.fori_loop(1, n, go, 0)

    def spread_drain(*how):
        def go(d, c):
            spread_copy(d, *how).wait_send()
            return c

        lax.fori_loop(1, n, go, 0)

    adj_copy = to_pair(0, adj.at[mine_rows], adj.at[mine_rows])
    cot_copy = to_pair(1, cot.at[:, other_cols], cot_all.at[mine_rows])
    halo = (halo_out, ext.at[pl.ds(nodes, n * nb)], nb, halo_send, halo_recv)
    spread_start(*halo)

    ext[pl.ds(0, nodes), :] = my_feat
    ext[pl.ds(pl.multiple_of(nodes + me * nb, nb), nb), :] = halo_out[at(me, nb), :]

    fresh = gru_rows(state[...], um[...], rm[...], ci[...], ch[...], ub[...], rb[...], cb[...])
    wt_mine[...] = fresh.astype(BF16)
    h = me // per_half
    place = lax.rem(me, per_half)

    def w_copy(i):
        d = 2 * i + r
        q = lax.rem(me + d, n)
        return d, pltpu.make_async_remote_copy(
            src_ref=wt_mine,
            dst_ref=wt.at[at(place, wrows)],
            send_sem=w_send.at[i],
            recv_sem=w_recv.at[place],
            device_id={"dom": q, "rep": h},
            device_id_type=MESH,
        )

    def w_start(i, c):
        d, copy = w_copy(i)

        @pl.when(d != 0)
        def _():
            copy.start()

        return c

    lax.fori_loop(0, n // 2, w_start, 0)

    @pl.when(h == r)
    def _():
        wt[at(place, wrows), :] = wt_mine[...]

    adj_copy.wait()
    full = adj[...]
    degree = jnp.sum(full.astype(F32), axis=1, keepdims=True)

    spread_wait(*halo)
    summed = dot(full, ext[...], NN)
    agg[:, mine_cols] = (summed / degree).astype(BF16)
    agg_copy = to_pair(2, agg.at[:, mine_cols], agg.at[:, mine_cols])

    def w_wait(i, c):
        src = r * per_half + i

        @pl.when(src != me)
        def _():
            pltpu.make_async_remote_copy(
                src_ref=wt_mine,
                dst_ref=wt.at[at(i, wrows)],
                send_sem=w_send.at[0],
                recv_sem=w_recv.at[i],
                device_id={"dom": src, "rep": other},
                device_id_type=MESH,
            ).wait_recv()

        return c

    lax.fori_loop(0, per_half, w_wait, 0)
    cot_copy.wait()
    agg_copy.wait()

    weights = wt[...]
    aggregated = agg[...]
    preact = dot(aggregated, weights, NT)
    sig = jax.nn.sigmoid(preact)
    grad_pre = (cot_all[...].astype(F32) * sig * (1.0 + preact * (1.0 - sig))).astype(BF16)
    mixed = dot(grad_pre, weights, NN)
    gm_out[...] = jnp.where(r == 0, mixed[:, half:], mixed[:, :half]).astype(BF16)
    mixed_mine = jnp.where(r == 0, mixed[:, :half], mixed[:, half:])
    gm_copy = to_pair(3, gm_out, gm_in)

    gw_out[...] = dot(aggregated, grad_pre, TN).astype(BF16)
    gw = (gw_out, gw_in, wrows, gw_send, gw_recv)

    gm_copy.wait()
    grad_summed = ((mixed_mine + gm_in[...].astype(F32)) / degree).astype(BF16)
    grad_halo = dot(full[:, nodes:], grad_summed, TN)
    ret_out[...] = grad_halo.astype(BF16)
    ret = (ret_out, ret_in, nb, ret_send, ret_recv)
    spread_start(*ret)
    spread_start(*gw)
    ret_in[at(me, nb), :] = ret_out[at(me, nb), :]
    gw_in[at(me, wrows), :] = gw_out[at(me, wrows), :]
    grad_local = dot(full[:, :nodes], grad_summed, TN)

    spread_wait(*ret)
    total = (grad_local + dot(picks, ret_in[...], NN)).astype(BF16)
    fin_out[...] = jnp.where(r == 0, total[TILE:], total[:TILE])
    fin_copy = to_pair(4, fin_out, fin_in)
    out_x[:, mine_cols] = jnp.where(r == 0, total[:TILE], total[TILE:])

    spread_wait(*gw)
    acc = gw_in[0:wrows, :].astype(F32)
    for p in range(1, n):
        acc = acc + gw_in[p * wrows : (p + 1) * wrows, :].astype(F32)
    gws_out[...] = jnp.where(r == 0, acc[wsplit:], acc[:wsplit])
    gws_copy = to_pair(5, gws_out, gws_in)
    out_w[:, mine_cols] = jnp.where(r == 0, acc[:wsplit], acc[wsplit:])

    fin_copy.wait()
    out_x[:, other_cols] = fin_in[...]
    gws_copy.wait()
    out_w[:, other_cols] = gws_in[...]

    def w_drain(i, c):
        d, copy = w_copy(i)

        @pl.when(d != 0)
        def _():
            copy.wait_send()

        return c

    lax.fori_loop(0, n // 2, w_drain, 0)
    spread_drain(*halo)
    spread_drain(*ret)
    spread_drain(*gw)


def local(
    features,
    tiles,
    tile_cols,
    tile_count,
    boundary_rows,
    boundary_count,
    cotangent,
    w_init,
    update_map,
    reset_map,
    cand_input,
    cand_hidden,
    update_bias,
    reset_bias,
    cand_bias,
):
    assert features.shape[0] == 1 and tiles.shape[1] == 1
    n = lax.axis_size("dom")
    nodes, width = features.shape[1:]
    half = width // 2
    nb = boundary_rows.shape[-1]
    kmax = tiles.shape[2]
    ncb = (nodes + n * nb) // TILE
    wrows = width // n
    maps = (update_map, reset_map, cand_input, cand_hidden)
    biases = (update_bias.T, reset_bias.T, cand_bias.T)
    state = w_init.T
    if lax.axis_size("snap") > 1:
        state = lax.fori_loop(
            0, lax.axis_index("snap"), lambda i, s: gru_rows(s, *maps, *biases), state
        )

    ks = jnp.arange(kmax, dtype=jnp.int32)
    hit = (tile_cols[0, 0][None, :] == jnp.arange(ncb, dtype=jnp.int32)[:, None]) & (
        ks < tile_count[0, 0]
    )[None, :]
    inv = jnp.sum(jnp.where(hit, ks[None, :], 0), axis=1)
    live = jnp.any(hit, axis=1).astype(F32)
    slots = jnp.arange(nb, dtype=jnp.int32)
    rowsel = jnp.where(slots[None, :] < boundary_count[0, 0][:, None], boundary_rows[0, 0], -1)
    rowsel = rowsel.reshape(1, n * nb)

    vmem = pl.BlockSpec(memory_space=pltpu.VMEM)
    smem = pl.BlockSpec(memory_space=pltpu.SMEM)
    dma = pltpu.SemaphoreType.DMA
    out_x, out_w = pl.pallas_call(
        functools.partial(kernel, n),
        out_shape=(
            jax.ShapeDtypeStruct((TILE, width), BF16),
            jax.ShapeDtypeStruct((wrows // 2, width), F32),
        ),
        in_specs=[vmem, vmem, smem, smem] + [vmem] * 10,
        out_specs=(vmem, vmem),
        scratch_shapes=[
            pltpu.VMEM((nodes, ncb * TILE), BF16),
            pltpu.VMEM((ncb * TILE, half), BF16),
            pltpu.VMEM((n * nb, half), BF16),
            pltpu.VMEM((nodes, half), BF16),
            pltpu.VMEM((wrows, width), BF16),
            pltpu.VMEM((half, width), BF16),
            pltpu.VMEM((nodes, width), BF16),
            pltpu.VMEM((nodes, half), BF16),
            pltpu.VMEM((nodes, half), BF16),
            pltpu.VMEM((n * nb, half), BF16),
            pltpu.VMEM((n * nb, half), BF16),
            pltpu.VMEM((width, half), BF16),
            pltpu.VMEM((width, half), BF16),
            pltpu.VMEM((wrows // 2, half), F32),
            pltpu.VMEM((wrows // 2, half), F32),
            pltpu.VMEM((TILE, half), BF16),
            pltpu.VMEM((TILE, half), BF16),
            dma((6,)),
            dma((6,)),
            dma((n,)),
            dma((n,)),
            dma((n // 2,)),
            dma((n // 2,)),
            dma((n,)),
            dma((n,)),
            dma((n,)),
            dma((n,)),
        ],
        compiler_params=pltpu.CompilerParams(
            collective_id=0, has_side_effects=True, vmem_limit_bytes=40 << 20
        ),
    )(features[0], tiles[0, 0], inv, live, rowsel, cotangent[0], state, *maps, *biases)
    return out_x[None], out_w[None]


def solution(mesh):
    in_specs = (
        P("snap", "dom", None),
        P("snap", ("dom", "rep"), None, None, None),
        P("snap", ("dom", "rep"), None),
        P("snap", ("dom", "rep")),
        P("snap", "dom", None, None),
        P("snap", "dom", None),
        P("snap", ("dom", "rep"), None),
        P(None, "dom"),
        P(),
        P(),
        P(),
        P(),
        P(None, "dom"),
        P(None, "dom"),
        P(None, "dom"),
    )
    out_specs = (P("snap", ("dom", "rep"), None), P("snap", ("dom", "rep"), None))
    return jax.shard_map(local, mesh=mesh, in_specs=in_specs, out_specs=out_specs, check_vma=False)
```

time: 231 us -> 51.6 us (0.22)
  waiting for transfers between devices: 128 us -> 0 us
  blocking collectives: 44.5 us -> 0 us
  Pallas kernels: 0 us -> 36.3 us
  between operations: 16.4 us -> 1.35 us
  starting transfers between devices: 13 us -> 0 us
  other arithmetic: 12.4 us -> 0.33 us
  matrix products: 4.63 us -> 0 us
    unnamed x3 -> x0, waiting for transfers between devices: 114 us -> none
    all_gather x1 -> x0, blocking collectives: 44.5 us -> none  [local(): lax.all_gather(stored.astype(jnp.bfloat16), 'dom', axis=2, tiled=True)]
    pallas_call x0 -> x1, Pallas kernels: none -> 36.3 us  [local(): pl.pallas_call(functools.partial(kernel, n), out_shape=(jax.ShapeDtypeStr...]
    all_to_all x2 -> x0, waiting for transfers between devices: 14.3 us -> none  [the longest x1 14.3 us: local(): lax.all_to_all(grad_halo, 'dom', split_axis=1, concat_axis=1, tiled=True)]
    all_to_all x2 -> x0, starting transfers between devices: 12.9 us -> none  [the longest x1 8.46 us: local(): lax.all_to_all(outgoing, 'dom', split_axis=1, concat_axis=1, tiled=True)]
    unnamed x29 -> x30, local copies, waits for them, and re-layouts: 1.78 us -> 12.8 us
    scatter-add x4 -> x0, other arithmetic: 6.69 us -> none  [the longest x2 3.82 us: add_rows(): return grad_part.at[indices.reshape(-1)].add(incoming.reshape(-1, width))]
    gather x4 -> x0, local copies, waits for them, and re-layouts: 4.95 us -> none  [pick_rows(): return source_rows[indices]]
  transfers between devices with their start and end apart: 4 -> 0, of which waited for: 2 -> 0; matrix products, arithmetic and copies ran while one was open for 5% -> 0% of each run, Pallas kernels for 0% -> 0%
where the time goes in v1:
time: 51.6 us; the launch traced here: 51 us
  Pallas kernels  36.3 us (70%)
  local copies, waits for them, and re-layouts  13 us (25%)
  between operations  1.35 us (3%)
    pallas_call x1, Pallas kernels, local(): pl.pallas_call(functools.partial(kernel, n), out_shape=(jax.ShapeDtypeStr...  36.3 us
    unnamed x30, local copies, waits for them, and re-layouts  12.8 us

profile of v1, /device:TPU:0, one launch (start us, length us, event | category | flops | bytes accessed | tf_op | source)
XLA Modules:
  0.0 51.0 jit_solution(15364456111287177461)
XLA Ops:
  1.3 0.0 copy-start.11
  1.3 0.0 copy-start.13
  1.3 0.7 %copy-done.13 = s32[1,1,6]{2,1,0:T(1,128)S(1)} copy-done((s32[1,1,6]{2,1,0:T(1,128)S(1)}, s32[1,1,6]{2,1,0:T(1,128)}, u32[]{:S(2)}) %copy-start.13) | copy-done | bytes 48
  2.0 0.1 fusion.1
  2.1 0.1 select_reduce_fusion.inv
  2.2 0.0 copy-done.11
  2.2 0.0 copy-start.12
  2.2 0.1 squeeze.18
  2.3 0.6 %copy-done.12 = s32[1,1,16]{2,1,0:T(1,128)S(1)} copy-done((s32[1,1,16]{2,1,0:T(1,128)S(1)}, s32[1,1,16]{2,1,0:T(1,128)}, u32[]{:S(2)}) %copy-start.12) | copy-done | bytes 88
  2.9 0.1 iota_compare_fusion
  2.9 0.1 lt.41
  3.0 0.0 copy-start
  3.1 1.0 %copy-done = bf16[512,512]{1,0:T(8,128)(2,1)S(1)} copy-done((bf16[512,512]{1,0:T(8,128)(2,1)S(1)}, bf16[512,512]{1,0:T(8,128)(2,1)}, u32[]{:S(2)}) %copy-start) | copy-done | bytes 524312
  4.1 0.0 copy-start.1
  4.1 1.0 %copy-done.1 = bf16[512,512]{1,0:T(8,128)(2,1)S(1)} copy-done((bf16[512,512]{1,0:T(8,128)(2,1)S(1)}, bf16[512,512]{1,0:T(8,128)(2,1)}, u32[]{:S(2)}) %copy-start.1) | copy-done | bytes 524312
  5.1 0.0 copy-start.2
  5.1 1.0 %copy-done.2 = bf16[512,512]{1,0:T(8,128)(2,1)S(1)} copy-done((bf16[512,512]{1,0:T(8,128)(2,1)S(1)}, bf16[512,512]{1,0:T(8,128)(2,1)}, u32[]{:S(2)}) %copy-start.2) | copy-done | bytes 524312
  6.2 0.0 copy-start.3
  6.2 1.0 %copy-done.3 = bf16[512,512]{1,0:T(8,128)(2,1)S(1)} copy-done((bf16[512,512]{1,0:T(8,128)(2,1)S(1)}, bf16[512,512]{1,0:T(8,128)(2,1)}, u32[]{:S(2)}) %copy-start.3) | copy-done | bytes 524312
  7.2 0.0 copy-start.4
  7.2 0.9 %copy-done.4 = bf16[1,256,512]{2,1,0:T(8,128)(2,1)S(1)} copy-done((bf16[1,256,512]{2,1,0:T(8,128)(2,1)S(1)}, bf16[1,256,512]{2,1,0:T(8,128)(2,1)}, u32[]{:S(2)}) %copy-start.4) | copy-done | bytes 262168
  8.2 0.0 copy-start.5
  8.2 0.9 %copy-done.5 = bf16[1,1,6,128,128]{4,3,2,1,0:T(8,128)(2,1)S(1)} copy-done((bf16[1,1,6,128,128]{4,3,2,1,0:T(8,128)(2,1)S(1)}, bf16[1,1,6,128,128]{4,3,2,1,0:T(8,128)(2,1)}, u32[]{:S(2)}) %copy-start.5) | copy-done | bytes 196632
  9.1 0.0 copy-start.6
  9.1 0.9 %copy-done.6 = bf16[1,128,512]{2,1,0:T(8,128)(2,1)S(1)} copy-done((bf16[1,128,512]{2,1,0:T(8,128)(2,1)S(1)}, bf16[1,128,512]{2,1,0:T(8,128)(2,1)}, u32[]{:S(2)}) %copy-start.6) | copy-done | bytes 131096
  10.0 0.0 copy-start.7
  10.0 0.8 %copy-done.7 = f32[512,32]{0,1:T(8,128)S(1)} copy-done((f32[512,32]{0,1:T(8,128)S(1)}, f32[512,32]{0,1:T(8,128)}, u32[]{:S(2)}) %copy-start.7) | copy-done | bytes 65560
  10.8 0.0 copy-start.8
  10.8 0.8 %copy-done.8 = f32[512,32]{0,1:T(8,128)S(1)} copy-done((f32[512,32]{0,1:T(8,128)S(1)}, f32[512,32]{0,1:T(8,128)}, u32[]{:S(2)}) %copy-start.8) | copy-done | bytes 65560
  11.7 0.0 copy-start.9
  11.7 0.8 %copy-done.9 = f32[512,32]{0,1:T(8,128)S(1)} copy-done((f32[512,32]{0,1:T(8,128)S(1)}, f32[512,32]{0,1:T(8,128)}, u32[]{:S(2)}) %copy-start.9) | copy-done | bytes 65560
  12.5 0.0 copy-start.10
  12.5 0.8 %copy-done.10 = f32[512,32]{0,1:T(8,128)S(1)} copy-done((f32[512,32]{0,1:T(8,128)S(1)}, f32[512,32]{0,1:T(8,128)}, u32[]{:S(2)}) %copy-start.10) | copy-done | bytes 65560
  13.4 36.3 %shard_map.158 = (bf16[128,512]{1,0:T(8,128)(2,1)S(1)}, f32[16,512]{1,0:T(8,128)S(1)}) custom-call(bf16[256,512]{1,0:T(8,128)(2,1)S(1)} %bitcast.15, bf16[6,128,128]{2,1,0:T(8,128)(2,1)S(1)} %bitcast.16, s32[6]{0:T(128)S(1)} %select_reduce_fusion.inv, f32[6]{0:T(128)S(1)} %convert_element_type.3.live, s32[1,512]{1,0:T(1,128)S(1)} %broadcast_select_fusion.rowsel, ...), custom_call_target="tpu_custom_call" | custom-call | tf_op jit(solution)/shard_map/pallas_call | solution.py:350
  49.7 0.7 %copy.20 = bf16[1,128,512]{2,1,0:T(8,128)(2,1)} copy(bf16[1,128,512]{2,1,0:T(8,128)(2,1)S(1)} %bitcast.18) | data formatting | bytes 262144
  50.4 0.6 %copy.21 = f32[1,16,512]{2,1,0:T(8,128)} copy(f32[1,16,512]{2,1,0:T(8,128)S(1)} %bitcast.23) | data formatting | bytes 65536
  (3 shorter events, 0.0 us)
Async XLA Ops:
  1.3 0.9 %copy-start.11 = (s32[1,1,16,32]{3,2,1,0:T(8,128)S(1)}, s32[1,1,16,32]{3,2,1,0:T(8,128)}, u32[]{:S(2)}) copy-start(s32[1,1,16,32]{3,2,1,0:T(8,128)} %param.19) | copy-start | bytes 6148
  1.3 0.7 %copy-start.13 = (s32[1,1,6]{2,1,0:T(1,128)S(1)}, s32[1,1,6]{2,1,0:T(1,128)}, u32[]{:S(2)}) copy-start(s32[1,1,6]{2,1,0:T(1,128)} %param.17) | copy-start | bytes 76
  2.2 0.7 %copy-start.12 = (s32[1,1,16]{2,1,0:T(1,128)S(1)}, s32[1,1,16]{2,1,0:T(1,128)}, u32[]{:S(2)}) copy-start(s32[1,1,16]{2,1,0:T(1,128)} %param.20) | copy-start | bytes 196
  3.0 1.0 %copy-start = (bf16[512,512]{1,0:T(8,128)(2,1)S(1)}, bf16[512,512]{1,0:T(8,128)(2,1)}, u32[]{:S(2)}) copy-start(bf16[512,512]{1,0:T(8,128)(2,1)} %um.1) | copy-start | bytes 1572868
  4.1 1.0 %copy-start.1 = (bf16[512,512]{1,0:T(8,128)(2,1)S(1)}, bf16[512,512]{1,0:T(8,128)(2,1)}, u32[]{:S(2)}) copy-start(bf16[512,512]{1,0:T(8,128)(2,1)} %rm.1) | copy-start | bytes 1572868
  5.1 1.0 %copy-start.2 = (bf16[512,512]{1,0:T(8,128)(2,1)S(1)}, bf16[512,512]{1,0:T(8,128)(2,1)}, u32[]{:S(2)}) copy-start(bf16[512,512]{1,0:T(8,128)(2,1)} %ci.1) | copy-start | bytes 1572868
  6.2 1.0 %copy-start.3 = (bf16[512,512]{1,0:T(8,128)(2,1)S(1)}, bf16[512,512]{1,0:T(8,128)(2,1)}, u32[]{:S(2)}) copy-start(bf16[512,512]{1,0:T(8,128)(2,1)} %ch.1) | copy-start | bytes 1572868
  7.2 0.9 %copy-start.4 = (bf16[1,256,512]{2,1,0:T(8,128)(2,1)S(1)}, bf16[1,256,512]{2,1,0:T(8,128)(2,1)}, u32[]{:S(2)}) copy-start(bf16[1,256,512]{2,1,0:T(8,128)(2,1)} %param.15) | copy-start | bytes 786436
  8.2 0.9 %copy-start.5 = (bf16[1,1,6,128,128]{4,3,2,1,0:T(8,128)(2,1)S(1)}, bf16[1,1,6,128,128]{4,3,2,1,0:T(8,128)(2,1)}, u32[]{:S(2)}) copy-start(bf16[1,1,6,128,128]{4,3,2,1,0:T(8,128)(2,1)} %param.16) | copy-start | bytes 589828
  9.1 0.9 %copy-start.6 = (bf16[1,128,512]{2,1,0:T(8,128)(2,1)S(1)}, bf16[1,128,512]{2,1,0:T(8,128)(2,1)}, u32[]{:S(2)}) copy-start(bf16[1,128,512]{2,1,0:T(8,128)(2,1)} %param.21) | copy-start | bytes 393220
  10.0 0.8 %copy-start.7 = (f32[512,32]{0,1:T(8,128)S(1)}, f32[512,32]{0,1:T(8,128)}, u32[]{:S(2)}) copy-start(f32[512,32]{0,1:T(8,128)} %param.22) | copy-start | bytes 196612
  10.8 0.8 %copy-start.8 = (f32[512,32]{0,1:T(8,128)S(1)}, f32[512,32]{0,1:T(8,128)}, u32[]{:S(2)}) copy-start(f32[512,32]{0,1:T(8,128)} %param.27) | copy-start | bytes 196612
  11.7 0.8 %copy-start.9 = (f32[512,32]{0,1:T(8,128)S(1)}, f32[512,32]{0,1:T(8,128)}, u32[]{:S(2)}) copy-start(f32[512,32]{0,1:T(8,128)} %param.28) | copy-start | bytes 196612
  12.5 0.8 %copy-start.10 = (f32[512,32]{0,1:T(8,128)S(1)}, f32[512,32]{0,1:T(8,128)}, u32[]{:S(2)}) copy-start(f32[512,32]{0,1:T(8,128)} %param.29) | copy-start | bytes 196612

commit v2 on v1

v2 whole, which is shorter than its diff:
```python
import functools

import jax
import jax.numpy as jnp
from jax import lax
from jax.experimental import pallas as pl
from jax.experimental.pallas import tpu as pltpu
from jax.sharding import PartitionSpec as P

TILE = 128
MESH = pl.DeviceIdType.MESH
F32 = jnp.float32
BF16 = jnp.bfloat16


def dot(a, b, dims):
    return lax.dot_general(a, b, (dims, ((), ())), preferred_element_type=F32)


NN = ((1,), (0,))
NT = ((1,), (1,))
TN = ((0,), (0,))


def gru_rows(state, um, rm, ci, ch, ub, rb, cb):
    state_bf = state.astype(BF16)
    update = jax.nn.sigmoid(dot(state_bf, um, NT) + ub)
    reset = jax.nn.sigmoid(dot(state_bf, rm, NT) + rb)
    gated = (reset * state).astype(BF16)
    candidate = jnp.tanh(dot(state_bf, ci, NT) + dot(gated, ch, NT) + cb)
    return (1.0 - update) * state + update * candidate


def kernel(
    n,
    lo,
    cols_ref,
    count_ref,
    *refs,
):
    (
        feat_hbm, tiles_hbm, brows_hbm, bcount_hbm, cot_hbm, state_hbm,
        um_hbm, rm_hbm, ci_hbm, ch_hbm, ub_hbm, rb_hbm, cb_hbm,
        out_x, out_w,
        feat, tiles, brows, bcount, cot, state, um, rm, ci, ch, ub, rb, cb,
        in_sem,
        picks, adj, ext, halo_out, cot_all, wt_mine, wt, agg, gm_out, gm_in,
        ret_out, ret_in, gw_out, gw1_in, gw_mid, gw2_in, gws_out, gws_in, fin_out, fin_in,
        pair_send, pair_recv, halo_send, halo_recv, w1_send, w2_send, w_recv,
        ret_send, ret_recv, gw1_send, gw1_recv, gw2_send, gw2_recv,
    ) = refs
    me = lax.axis_index("dom")
    r = lax.axis_index("rep")
    other = 1 - r
    hi = n // lo
    z, l = me // lo, lax.rem(me, lo)
    nodes, width = feat.shape
    half = width // 2
    nb = brows.shape[1]
    wrows = wt_mine.shape[0]
    kmax = tiles.shape[0]
    ncb = adj.shape[1] // TILE
    wsplit = gws_out.shape[0]

    hbm = (feat_hbm, brows_hbm, bcount_hbm, tiles_hbm, cot_hbm, state_hbm,
           um_hbm, rm_hbm, ci_hbm, ch_hbm, ub_hbm, rb_hbm, cb_hbm)
    vmem = (feat, brows, bcount, tiles, cot, state, um, rm, ci, ch, ub, rb, cb)
    loads = [pltpu.make_async_copy(x, y, in_sem.at[i]) for i, (x, y) in enumerate(zip(hbm, vmem))]
    for load in loads:
        load.start()

    def cols(which):
        return pl.ds(pl.multiple_of(which * half, half), half)

    def at(i, size):
        return pl.ds(pl.multiple_of(i * size, size), size)

    def remote(src, dst, send_sem, recv_sem, dom, rep):
        return pltpu.make_async_remote_copy(
            src_ref=src,
            dst_ref=dst,
            send_sem=send_sem,
            recv_sem=recv_sem,
            device_id={"dom": dom, "rep": rep},
            device_id_type=MESH,
        )

    mine_rows = at(r, TILE)
    mine_cols, other_cols = cols(r), cols(other)

    barrier = pltpu.get_barrier_semaphore()

    def greet(i, c):
        q = lax.rem(me + i, n)
        pl.semaphore_signal(barrier, inc=1, device_id={"dom": q, "rep": other}, device_id_type=MESH)

        @pl.when(i != 0)
        def _():
            pl.semaphore_signal(barrier, inc=1, device_id={"dom": q, "rep": r}, device_id_type=MESH)

        return c

    lax.fori_loop(0, n, greet, 0)

    for load in loads[:3]:
        load.wait()
    lane = lax.broadcasted_iota(jnp.int32, (nb, n * nb), 1)
    spread_slot = (lax.rem(lane, nb) == lax.broadcasted_iota(jnp.int32, (nb, n * nb), 0)).astype(F32)
    lane_q = lax.broadcasted_iota(jnp.int32, (n, n * nb), 1)
    in_q = lax.div(lane_q, nb) == lax.broadcasted_iota(jnp.int32, (n, n * nb), 0)
    by_slot = dot(brows[...].astype(F32).astype(BF16), spread_slot.astype(BF16), NN)
    row_of = jnp.sum(jnp.where(in_q, by_slot, 0.0), axis=0, keepdims=True)
    counts = jnp.broadcast_to(bcount[...].astype(F32), (n, n)).astype(BF16)
    limit = dot(counts, in_q.astype(F32).astype(BF16), NN)[0:1]
    slot = lax.rem(lane_q[0:1], nb).astype(F32)
    rowsel = jnp.where(slot < limit, row_of, -1.0).astype(jnp.int32)
    picks[...] = (lax.broadcasted_iota(jnp.int32, (nodes, n * nb), 0) == rowsel).astype(F32).astype(BF16)
    halo_out[...] = dot(picks[...], feat[:, mine_cols], TN).astype(BF16)

    for load in loads[3:5]:
        load.wait()
    for c in range(ncb):
        index = jnp.int32(0)
        live = jnp.float32(0.0)
        for k in range(kmax):
            hit = (cols_ref[0, k] == c) & (k < count_ref[0, 0])
            index = jnp.where(hit, k, index)
            live = jnp.where(hit, 1.0, live)
        adj[mine_rows, c * TILE : (c + 1) * TILE] = (tiles[index].astype(F32) * live).astype(BF16)
    cot_all[mine_rows, :] = cot[:, mine_cols]

    pl.semaphore_wait(barrier, 2 * n - 1)

    def to_pair(slot, src, dst):
        copy = remote(src, dst, pair_send.at[slot], pair_recv.at[slot], me, other)
        copy.start()
        return copy

    def spread_copy(d, out_ref, in_ref, send_sem, recv_sem):
        q = lax.rem(me + d, n)
        return remote(
            out_ref.at[at(q, nb)], in_ref.at[at(me, nb)], send_sem.at[d], recv_sem.at[d], q, r
        )

    def spread_start(*how):
        def go(d, c):
            spread_copy(d, *how).start()
            return c

        lax.fori_loop(1, n, go, 0)

    def spread_wait(out_ref, in_ref, send_sem, recv_sem):
        def go(d, c):
            src = lax.rem(me + n - d, n)
            block = at(src, nb)
            remote(
                out_ref.at[block], in_ref.at[block], send_sem.at[d], recv_sem.at[d], src, r
            ).wait_recv()
            return c

        lax.fori_loop(1, n, go, 0)

    def spread_drain(*how):
        def go(d, c):
            spread_copy(d, *how).wait_send()
            return c

        lax.fori_loop(1, n, go, 0)

    halo = (halo_out, ext.at[pl.ds(nodes, n * nb)], halo_send, halo_recv)
    spread_start(*halo)
    adj_copy = to_pair(0, adj.at[mine_rows], adj.at[mine_rows])
    cot_copy = to_pair(1, cot.at[:, other_cols], cot_all.at[mine_rows])

    for load in loads[5:]:
        load.wait()
    fresh = gru_rows(state[...], um[...], rm[...], ci[...], ch[...], ub[...], rb[...], cb[...])
    wt_mine[...] = fresh.astype(BF16)
    zh = hi // 2
    h = z // zh
    place = lax.rem(z, zh) * lo + l

    def w1_copy(i):
        dz = 2 * i + r
        q = lax.rem(z + dz, hi) * lo + l
        return dz, remote(
            wt_mine, wt.at[at(place, wrows)], w1_send.at[i], w_recv.at[place], q, h
        )

    for i in range(zh):
        dz, copy = w1_copy(i)

        @pl.when(dz != 0)
        def _():
            copy.start()

    @pl.when(h == r)
    def _():
        wt[at(place, wrows), :] = wt_mine[...]

    ext[pl.ds(0, nodes), :] = feat[:, mine_cols]
    ext[pl.ds(pl.multiple_of(nodes + me * nb, nb), nb), :] = halo_out[at(me, nb), :]

    adj_copy.wait()
    degree = jnp.sum(adj[...].astype(F32), axis=1, keepdims=True)

    def w_arrival(block):
        here = wt.at[at(block, wrows)]
        return remote(here, here, w1_send.at[0], w_recv.at[block], me, other)

    def w2_copy(i, dl):
        block = i * lo + l
        here = wt.at[at(block, wrows)]
        q = z * lo + lax.rem(l + dl, lo)
        return remote(here, here, w2_send.at[i * lo + dl], w_recv.at[block], q, r)

    for i in range(zh):

        @pl.when(r * zh + i != z)
        def _():
            w_arrival(i * lo + l).wait_recv()

        for dl in range(1, lo):
            w2_copy(i, dl).start()

    spread_wait(*halo)
    agg[:, mine_cols] = (dot(adj[...], ext[...], NN) / degree).astype(BF16)
    agg_copy = to_pair(2, agg.at[:, mine_cols], agg.at[:, mine_cols])

    for i in range(zh):
        for dl in range(1, lo):
            w_arrival(i * lo + lax.rem(l + dl, lo)).wait_recv()
    cot_copy.wait()
    agg_copy.wait()

    preact = dot(agg[...], wt[...], NT)
    sig = jax.nn.sigmoid(preact)
    grad_pre = (cot_all[...].astype(F32) * sig * (1.0 + preact * (1.0 - sig))).astype(BF16)
    mixed = dot(grad_pre, wt[...], NN)
    gm_out[...] = jnp.where(r == 0, mixed[:, half:], mixed[:, :half]).astype(BF16)
    mixed_mine = jnp.where(r == 0, mixed[:, :half], mixed[:, half:])
    gm_copy = to_pair(3, gm_out, gm_in)

    partial = dot(agg[...], grad_pre, TN)
    for p in range(n):
        to = ((p % lo) * hi + p // lo) * wrows
        gw_out[to : to + wrows, :] = partial[p * wrows : (p + 1) * wrows].astype(BF16)
    rows1 = hi * wrows

    def gw1_copy(dl):
        to = lax.rem(l + dl, lo)
        return remote(
            gw_out.at[at(to, rows1)], gw1_in.at[dl], gw1_send.at[dl], gw1_recv.at[dl], z * lo + to, r
        )

    def gw2_copy(dz):
        to = lax.rem(z + dz, hi)
        return remote(
            gw_mid.at[at(to, wrows)], gw2_in.at[dz], gw2_send.at[dz], gw2_recv.at[dz], to * lo + l, r
        )

    gm_copy.wait()
    grad_summed = ((mixed_mine + gm_in[...].astype(F32)) / degree).astype(BF16)
    ret_out[...] = dot(adj[:, nodes:], grad_summed, TN).astype(BF16)
    ret = (ret_out, ret_in, ret_send, ret_recv)
    spread_start(*ret)
    for dl in range(1, lo):
        gw1_copy(dl).start()
    ret_in[at(me, nb), :] = ret_out[at(me, nb), :]
    grad_local = dot(adj[:, :nodes], grad_summed, TN)

    acc = gw_out[at(l, rows1), :].astype(F32)
    for dl in range(1, lo):
        gw1_copy(dl).wait_recv()
        acc = acc + gw1_in[dl].astype(F32)
    gw_mid[...] = acc.astype(BF16)
    for dz in range(1, hi):
        gw2_copy(dz).start()

    spread_wait(*ret)
    total = (grad_local + dot(picks[...], ret_in[...], NN)).astype(BF16)
    fin_out[...] = jnp.where(r == 0, total[TILE:], total[:TILE])
    fin_copy = to_pair(4, fin_out, fin_in)
    out_x[:, mine_cols] = jnp.where(r == 0, total[:TILE], total[TILE:])

    acc = gw_mid[at(z, wrows), :].astype(F32)
    for dz in range(1, hi):
        gw2_copy(dz).wait_recv()
        acc = acc + gw2_in[dz].astype(F32)
    gws_out[...] = jnp.where(r == 0, acc[wsplit:], acc[:wsplit])
    gws_copy = to_pair(5, gws_out, gws_in)
    out_w[:, mine_cols] = jnp.where(r == 0, acc[:wsplit], acc[wsplit:])

    fin_copy.wait()
    out_x[:, other_cols] = fin_in[...]
    gws_copy.wait()
    out_w[:, other_cols] = gws_in[...]

    for i in range(zh):
        dz, copy = w1_copy(i)

        @pl.when(dz != 0)
        def _():
            copy.wait_send()

        for dl in range(1, lo):
            w2_copy(i, dl).wait_send()
    for dl in range(1, lo):
        gw1_copy(dl).wait_send()
    for dz in range(1, hi):
        gw2_copy(dz).wait_send()
    spread_drain(*halo)
    spread_drain(*ret)


def local(
    features,
    tiles,
    tile_cols,
    tile_count,
    boundary_rows,
    boundary_count,
    cotangent,
    w_init,
    update_map,
    reset_map,
    cand_input,
    cand_hidden,
    update_bias,
    reset_bias,
    cand_bias,
):
    assert features.shape[0] == 1 and tiles.shape[1] == 1
    n = lax.axis_size("dom")
    nodes, width = features.shape[1:]
    half = width // 2
    nb = boundary_rows.shape[-1]
    ncb = (nodes + n * nb) // TILE
    wrows = width // n
    maps = (update_map, reset_map, cand_input, cand_hidden)
    biases = (update_bias.T, reset_bias.T, cand_bias.T)
    state = w_init.T
    if lax.axis_size("snap") > 1:
        state = lax.fori_loop(
            0, lax.axis_index("snap"), lambda i, s: gru_rows(s, *maps, *biases), state
        )

    lo = 4
    hi = n // lo
    zh = hi // 2
    arrays = (features[0], tiles[0, 0], boundary_rows[0, 0], boundary_count[0], cotangent[0], state)
    arrays = arrays + maps + biases
    hbm = pl.BlockSpec(memory_space=pltpu.HBM)
    vmem = pl.BlockSpec(memory_space=pltpu.VMEM)
    smem = pl.BlockSpec(memory_space=pltpu.SMEM)
    dma = pltpu.SemaphoreType.DMA
    out_x, out_w = pl.pallas_call(
        functools.partial(kernel, n, lo),
        out_shape=(
            jax.ShapeDtypeStruct((TILE, width), BF16),
            jax.ShapeDtypeStruct((wrows // 2, width), F32),
        ),
        in_specs=[smem, smem] + [hbm] * len(arrays),
        out_specs=(vmem, vmem),
        scratch_shapes=[pltpu.VMEM(x.shape, x.dtype) for x in arrays]
        + [
            dma((len(arrays),)),
            pltpu.VMEM((nodes, n * nb), BF16),
            pltpu.VMEM((nodes, ncb * TILE), BF16),
            pltpu.VMEM((ncb * TILE, half), BF16),
            pltpu.VMEM((n * nb, half), BF16),
            pltpu.VMEM((nodes, half), BF16),
            pltpu.VMEM((wrows, width), BF16),
            pltpu.VMEM((half, width), BF16),
            pltpu.VMEM((nodes, width), BF16),
            pltpu.VMEM((nodes, half), BF16),
            pltpu.VMEM((nodes, half), BF16),
            pltpu.VMEM((n * nb, half), BF16),
            pltpu.VMEM((n * nb, half), BF16),
            pltpu.VMEM((width, half), BF16),
            pltpu.VMEM((lo, hi * wrows, half), BF16),
            pltpu.VMEM((hi * wrows, half), BF16),
            pltpu.VMEM((hi, wrows, half), BF16),
            pltpu.VMEM((wrows // 2, half), F32),
            pltpu.VMEM((wrows // 2, half), F32),
            pltpu.VMEM((TILE, half), BF16),
            pltpu.VMEM((TILE, half), BF16),
            dma((6,)),
            dma((6,)),
            dma((n,)),
            dma((n,)),
            dma((zh,)),
            dma((zh * lo,)),
            dma((zh * lo,)),
            dma((n,)),
            dma((n,)),
            dma((lo,)),
            dma((lo,)),
            dma((hi,)),
            dma((hi,)),
        ],
        compiler_params=pltpu.CompilerParams(
            collective_id=0, has_side_effects=True, vmem_limit_bytes=40 << 20
        ),
    )(tile_cols[0], tile_count, *arrays)
    return out_x[None], out_w[None]


def solution(mesh):
    in_specs = (
        P("snap", "dom", None),
        P("snap", ("dom", "rep"), None, None, None),
        P("snap", ("dom", "rep"), None),
        P("snap", ("dom", "rep")),
        P("snap", "dom", None, None),
        P("snap", "dom", None),
        P("snap", ("dom", "rep"), None),
        P(None, "dom"),
        P(),
        P(),
        P(),
        P(),
        P(None, "dom"),
        P(None, "dom"),
        P(None, "dom"),
    )
    out_specs = (P("snap", ("dom", "rep"), None), P("snap", ("dom", "rep"), None))
    return jax.shard_map(local, mesh=mesh, in_specs=in_specs, out_specs=out_specs, check_vma=False)
```

time: 51.6 us -> 50.4 us (0.977)
  local copies, waits for them, and re-layouts: 13 us -> 12.3 us
    unnamed x30, local copies, waits for them, and re-layouts: 12.8 us -> 12.3 us
where the time goes in v2:
time: 50.4 us; the launch traced here: 49.8 us
  Pallas kernels  36.2 us (72%)
  local copies, waits for them, and re-layouts  12.3 us (24%)
  between operations  1.33 us (3%)
    pallas_call x1, Pallas kernels, local(): pl.pallas_call(functools.partial(kernel, n, lo), out_shape=(jax.ShapeDtyp...  36.2 us
    unnamed x30, local copies, waits for them, and re-layouts  12.3 us

profile of v2, /device:TPU:0, one launch (start us, length us, event | category | flops | bytes accessed | tf_op | source)
XLA Modules:
  0.0 49.8 jit_solution(17638003358719998559)
XLA Ops:
  1.3 0.0 copy-start.11
  1.3 0.0 copy-start.12
  1.3 0.0 copy-start.13
  1.3 0.7 %copy-done.11 = s32[1,1,16,32]{3,2,1,0:T(8,128)S(1)} copy-done((s32[1,1,16,32]{3,2,1,0:T(8,128)S(1)}, s32[1,1,16,32]{3,2,1,0:T(8,128)}, u32[]{:S(2)}) %copy-start.11) | copy-done | bytes 2072
  2.0 0.0 copy-done.12
  2.0 0.0 copy-done.13
  2.0 0.0 copy-start
  2.0 1.0 %copy-done = bf16[512,512]{1,0:T(8,128)(2,1)S(1)} copy-done((bf16[512,512]{1,0:T(8,128)(2,1)S(1)}, bf16[512,512]{1,0:T(8,128)(2,1)}, u32[]{:S(2)}) %copy-start) | copy-done | bytes 524312
  3.0 0.0 copy-start.1
  3.0 1.0 %copy-done.1 = bf16[512,512]{1,0:T(8,128)(2,1)S(1)} copy-done((bf16[512,512]{1,0:T(8,128)(2,1)S(1)}, bf16[512,512]{1,0:T(8,128)(2,1)}, u32[]{:S(2)}) %copy-start.1) | copy-done | bytes 524312
  4.1 0.0 copy-start.2
  4.1 1.0 %copy-done.2 = bf16[512,512]{1,0:T(8,128)(2,1)S(1)} copy-done((bf16[512,512]{1,0:T(8,128)(2,1)S(1)}, bf16[512,512]{1,0:T(8,128)(2,1)}, u32[]{:S(2)}) %copy-start.2) | copy-done | bytes 524312
  5.1 0.0 copy-start.3
  5.1 1.0 %copy-done.3 = bf16[512,512]{1,0:T(8,128)(2,1)S(1)} copy-done((bf16[512,512]{1,0:T(8,128)(2,1)S(1)}, bf16[512,512]{1,0:T(8,128)(2,1)}, u32[]{:S(2)}) %copy-start.3) | copy-done | bytes 524312
  6.2 0.0 copy-start.4
  6.2 0.9 %copy-done.4 = bf16[1,256,512]{2,1,0:T(8,128)(2,1)S(1)} copy-done((bf16[1,256,512]{2,1,0:T(8,128)(2,1)S(1)}, bf16[1,256,512]{2,1,0:T(8,128)(2,1)}, u32[]{:S(2)}) %copy-start.4) | copy-done | bytes 262168
  7.1 0.0 copy-start.5
  7.1 0.9 %copy-done.5 = bf16[1,1,6,128,128]{4,3,2,1,0:T(8,128)(2,1)S(1)} copy-done((bf16[1,1,6,128,128]{4,3,2,1,0:T(8,128)(2,1)S(1)}, bf16[1,1,6,128,128]{4,3,2,1,0:T(8,128)(2,1)}, u32[]{:S(2)}) %copy-start.5) | copy-done | bytes 196632
  8.0 0.0 copy-start.6
  8.0 0.9 %copy-done.6 = bf16[1,128,512]{2,1,0:T(8,128)(2,1)S(1)} copy-done((bf16[1,128,512]{2,1,0:T(8,128)(2,1)S(1)}, bf16[1,128,512]{2,1,0:T(8,128)(2,1)}, u32[]{:S(2)}) %copy-start.6) | copy-done | bytes 131096
  8.9 0.0 copy-start.7
  8.9 0.8 %copy-done.7 = f32[512,32]{0,1:T(8,128)S(1)} copy-done((f32[512,32]{0,1:T(8,128)S(1)}, f32[512,32]{0,1:T(8,128)}, u32[]{:S(2)}) %copy-start.7) | copy-done | bytes 65560
  9.8 0.0 copy-start.8
  9.8 0.8 %copy-done.8 = f32[512,32]{0,1:T(8,128)S(1)} copy-done((f32[512,32]{0,1:T(8,128)S(1)}, f32[512,32]{0,1:T(8,128)}, u32[]{:S(2)}) %copy-start.8) | copy-done | bytes 65560
  10.6 0.0 copy-start.9
  10.6 0.8 %copy-done.9 = f32[512,32]{0,1:T(8,128)S(1)} copy-done((f32[512,32]{0,1:T(8,128)S(1)}, f32[512,32]{0,1:T(8,128)}, u32[]{:S(2)}) %copy-start.9) | copy-done | bytes 65560
  11.5 0.0 copy-start.10
  11.5 0.8 %copy-done.10 = f32[512,32]{0,1:T(8,128)S(1)} copy-done((f32[512,32]{0,1:T(8,128)S(1)}, f32[512,32]{0,1:T(8,128)}, u32[]{:S(2)}) %copy-start.10) | copy-done | bytes 65560
  12.3 36.2 %shard_map.158 = (bf16[128,512]{1,0:T(8,128)(2,1)S(1)}, f32[16,512]{1,0:T(8,128)S(1)}) custom-call(s32[1,6]{1,0:T(1,128)S(1)} %bitcast.22, s32[1,1]{1,0:T(1,128)S(6)} %copy.19.count_ref, bf16[256,512]{1,0:T(8,128)(2,1)S(1)} %bitcast.12, bf16[6,128,128]{2,1,0:T(8,128)(2,1)S(1)} %bitcast.13, s32[16,32]{1,0:T(8,128)S(1)} %bitcast.21, s32[1,16]{1,0:T(1,128)S(1)} %bitcast.23, ...), custom_call_target="tpu_custom_call" | custom-call | tf_op jit(solution)/shard_map/pallas_call | solution.py:357
  48.5 0.7 %copy.20 = bf16[1,128,512]{2,1,0:T(8,128)(2,1)} copy(bf16[1,128,512]{2,1,0:T(8,128)(2,1)S(1)} %bitcast.15) | data formatting | bytes 262144
  49.1 0.6 %copy.21 = f32[1,16,512]{2,1,0:T(8,128)} copy(f32[1,16,512]{2,1,0:T(8,128)S(1)} %bitcast.20) | data formatting | bytes 65536
Async XLA Ops:
  1.3 0.7 %copy-start.11 = (s32[1,1,16,32]{3,2,1,0:T(8,128)S(1)}, s32[1,1,16,32]{3,2,1,0:T(8,128)}, u32[]{:S(2)}) copy-start(s32[1,1,16,32]{3,2,1,0:T(8,128)} %param.19) | copy-start | bytes 6148
  1.3 0.7 %copy-start.12 = (s32[1,1,6]{2,1,0:T(1,128)S(1)}, s32[1,1,6]{2,1,0:T(1,128)}, u32[]{:S(2)}) copy-start(s32[1,1,6]{2,1,0:T(1,128)} %param.17) | copy-start | bytes 76
  1.3 0.7 %copy-start.13 = (s32[1,1,16]{2,1,0:T(1,128)S(1)}, s32[1,1,16]{2,1,0:T(1,128)}, u32[]{:S(2)}) copy-start(s32[1,1,16]{2,1,0:T(1,128)} %param.20) | copy-start | bytes 196
  2.0 1.0 %copy-start = (bf16[512,512]{1,0:T(8,128)(2,1)S(1)}, bf16[512,512]{1,0:T(8,128)(2,1)}, u32[]{:S(2)}) copy-start(bf16[512,512]{1,0:T(8,128)(2,1)} %refs_6_.1) | copy-start | bytes 1572868
  3.0 1.0 %copy-start.1 = (bf16[512,512]{1,0:T(8,128)(2,1)S(1)}, bf16[512,512]{1,0:T(8,128)(2,1)}, u32[]{:S(2)}) copy-start(bf16[512,512]{1,0:T(8,128)(2,1)} %refs_7_.1) | copy-start | bytes 1572868
  4.1 1.0 %copy-start.2 = (bf16[512,512]{1,0:T(8,128)(2,1)S(1)}, bf16[512,512]{1,0:T(8,128)(2,1)}, u32[]{:S(2)}) copy-start(bf16[512,512]{1,0:T(8,128)(2,1)} %refs_8_.1) | copy-start | bytes 1572868
  5.1 1.0 %copy-start.3 = (bf16[512,512]{1,0:T(8,128)(2,1)S(1)}, bf16[512,512]{1,0:T(8,128)(2,1)}, u32[]{:S(2)}) copy-start(bf16[512,512]{1,0:T(8,128)(2,1)} %refs_9_.1) | copy-start | bytes 1572868
  6.2 0.9 %copy-start.4 = (bf16[1,256,512]{2,1,0:T(8,128)(2,1)S(1)}, bf16[1,256,512]{2,1,0:T(8,128)(2,1)}, u32[]{:S(2)}) copy-start(bf16[1,256,512]{2,1,0:T(8,128)(2,1)} %param.15) | copy-start | bytes 786436
  7.1 0.9 %copy-start.5 = (bf16[1,1,6,128,128]{4,3,2,1,0:T(8,128)(2,1)S(1)}, bf16[1,1,6,128,128]{4,3,2,1,0:T(8,128)(2,1)}, u32[]{:S(2)}) copy-start(bf16[1,1,6,128,128]{4,3,2,1,0:T(8,128)(2,1)} %param.16) | copy-start | bytes 589828
  8.0 0.9 %copy-start.6 = (bf16[1,128,512]{2,1,0:T(8,128)(2,1)S(1)}, bf16[1,128,512]{2,1,0:T(8,128)(2,1)}, u32[]{:S(2)}) copy-start(bf16[1,128,512]{2,1,0:T(8,128)(2,1)} %param.21) | copy-start | bytes 393220
  8.9 0.8 %copy-start.7 = (f32[512,32]{0,1:T(8,128)S(1)}, f32[512,32]{0,1:T(8,128)}, u32[]{:S(2)}) copy-start(f32[512,32]{0,1:T(8,128)} %param.22) | copy-start | bytes 196612
  9.8 0.8 %copy-start.8 = (f32[512,32]{0,1:T(8,128)S(1)}, f32[512,32]{0,1:T(8,128)}, u32[]{:S(2)}) copy-start(f32[512,32]{0,1:T(8,128)} %param.27) | copy-start | bytes 196612
  10.6 0.8 %copy-start.9 = (f32[512,32]{0,1:T(8,128)S(1)}, f32[512,32]{0,1:T(8,128)}, u32[]{:S(2)}) copy-start(f32[512,32]{0,1:T(8,128)} %param.28) | copy-start | bytes 196612
  11.5 0.8 %copy-start.10 = (f32[512,32]{0,1:T(8,128)S(1)}, f32[512,32]{0,1:T(8,128)}, u32[]{:S(2)}) copy-start(f32[512,32]{0,1:T(8,128)} %param.29) | copy-start | bytes 196612

commit v3 on v2

--- a/solution.py
+++ b/solution.py
@@ -90,17 +90,14 @@
 
     barrier = pltpu.get_barrier_semaphore()
 
+    pl.semaphore_signal(barrier, inc=1, device_id={"dom": me, "rep": other}, device_id_type=MESH)
+
     def greet(i, c):
         q = lax.rem(me + i, n)
-        pl.semaphore_signal(barrier, inc=1, device_id={"dom": q, "rep": other}, device_id_type=MESH)
-
-        @pl.when(i != 0)
-        def _():
-            pl.semaphore_signal(barrier, inc=1, device_id={"dom": q, "rep": r}, device_id_type=MESH)
-
+        pl.semaphore_signal(barrier, inc=1, device_id={"dom": q, "rep": r}, device_id_type=MESH)
         return c
 
-    lax.fori_loop(0, n, greet, 0)
+    lax.fori_loop(1, n, greet, 0)
 
     for load in loads[:3]:
         load.wait()
@@ -129,7 +126,12 @@
         adj[mine_rows, c * TILE : (c + 1) * TILE] = (tiles[index].astype(F32) * live).astype(BF16)
     cot_all[mine_rows, :] = cot[:, mine_cols]
 
-    pl.semaphore_wait(barrier, 2 * n - 1)
+    for load in loads[5:]:
+        load.wait()
+    fresh = gru_rows(state[...], um[...], rm[...], ci[...], ch[...], ub[...], rb[...], cb[...])
+    wt_mine[...] = fresh.astype(BF16)
+
+    pl.semaphore_wait(barrier, n)
 
     def to_pair(slot, src, dst):
         copy = remote(src, dst, pair_send.at[slot], pair_recv.at[slot], me, other)
@@ -168,36 +170,26 @@
         lax.fori_loop(1, n, go, 0)
 
     halo = (halo_out, ext.at[pl.ds(nodes, n * nb)], halo_send, halo_recv)
-    spread_start(*halo)
     adj_copy = to_pair(0, adj.at[mine_rows], adj.at[mine_rows])
     cot_copy = to_pair(1, cot.at[:, other_cols], cot_all.at[mine_rows])
 
-    for load in loads[5:]:
-        load.wait()
-    fresh = gru_rows(state[...], um[...], rm[...], ci[...], ch[...], ub[...], rb[...], cb[...])
-    wt_mine[...] = fresh.astype(BF16)
     zh = hi // 2
     h = z // zh
     place = lax.rem(z, zh) * lo + l
 
-    def w1_copy(i):
-        dz = 2 * i + r
+    def w1_copy(dz):
         q = lax.rem(z + dz, hi) * lo + l
-        return dz, remote(
-            wt_mine, wt.at[at(place, wrows)], w1_send.at[i], w_recv.at[place], q, h
-        )
-
-    for i in range(zh):
-        dz, copy = w1_copy(i)
-
-        @pl.when(dz != 0)
-        def _():
-            copy.start()
+        return remote(
+            wt_mine, wt.at[at(place, wrows)], w1_send.at[dz], w_recv.at[place], q, r
+        )
 
     @pl.when(h == r)
     def _():
+        for dz in range(1, hi):
+            w1_copy(dz).start()
         wt[at(place, wrows), :] = wt_mine[...]
 
+    spread_start(*halo)
     ext[pl.ds(0, nodes), :] = feat[:, mine_cols]
     ext[pl.ds(pl.multiple_of(nodes + me * nb, nb), nb), :] = halo_out[at(me, nb), :]
 
@@ -259,13 +251,14 @@
             gw_mid.at[at(to, wrows)], gw2_in.at[dz], gw2_send.at[dz], gw2_recv.at[dz], to * lo + l, r
         )
 
+    for dl in range(1, lo):
+        gw1_copy(dl).start()
+
     gm_copy.wait()
     grad_summed = ((mixed_mine + gm_in[...].astype(F32)) / degree).astype(BF16)
     ret_out[...] = dot(adj[:, nodes:], grad_summed, TN).astype(BF16)
     ret = (ret_out, ret_in, ret_send, ret_recv)
     spread_start(*ret)
-    for dl in range(1, lo):
-        gw1_copy(dl).start()
     ret_in[at(me, nb), :] = ret_out[at(me, nb), :]
     grad_local = dot(adj[:, :nodes], grad_summed, TN)
 
@@ -296,13 +289,12 @@
     gws_copy.wait()
     out_w[:, other_cols] = gws_in[...]
 
+    @pl.when(h == r)
+    def _():
+        for dz in range(1, hi):
+            w1_copy(dz).wait_send()
+
     for i in range(zh):
-        dz, copy = w1_copy(i)
-
-        @pl.when(dz != 0)
-        def _():
-            copy.wait_send()
-
         for dl in range(1, lo):
             w2_copy(i, dl).wait_send()
     for dl in range(1, lo):
@@ -389,7 +381,7 @@
             dma((6,)),
             dma((n,)),
             dma((n,)),
-            dma((zh,)),
+            dma((hi,)),
             dma((zh * lo,)),
             dma((zh * lo,)),
             dma((n,)),
@@ -400,7 +392,7 @@
             dma((hi,)),
         ],
         compiler_params=pltpu.CompilerParams(
-            collective_id=0, has_side_effects=True, vmem_limit_bytes=40 << 20
+            collective_id=0, has_side_effects=True, vmem_limit_bytes=60 << 20
         ),
     )(tile_cols[0], tile_count, *arrays)
     return out_x[None], out_w[None]

time: 50.4 us -> 34.9 us (0.69)
  local copies, waits for them, and re-layouts: 12.3 us -> 2.19 us
  Pallas kernels: 36.2 us -> 31.3 us
    unnamed x30 -> x4, local copies, waits for them, and re-layouts: 12.3 us -> 2.19 us
    pallas_call x1, Pallas kernels: 36.2 us -> 31.3 us  [local(): pl.pallas_call(functools.partial(kernel, n, lo), out_shape=(jax.ShapeDtyp...]
where the time goes in v3:
time: 34.9 us; the launch traced here: 34.7 us
  Pallas kernels  31.3 us (90%)
  local copies, waits for them, and re-layouts  2.19 us (6%)
  between operations  1.3 us (4%)
    pallas_call x1, Pallas kernels, local(): pl.pallas_call(functools.partial(kernel, n, lo), out_shape=(jax.ShapeDtyp...  31.3 us
    unnamed x4, local copies, waits for them, and re-layouts  2.19 us

profile of v3, /device:TPU:0, one launch (start us, length us, event | category | flops | bytes accessed | tf_op | source)
XLA Modules:
  0.0 34.7 jit_solution(16425934807999882736)
XLA Ops:
  1.3 31.3 %shard_map.158 = (bf16[128,512]{1,0:T(8,128)(2,1)}, f32[16,512]{1,0:T(8,128)}) custom-call(s32[1,6]{1,0:T(1,128)} %bitcast.22, s32[1,1]{1,0:T(1,128)S(6)} %copy.19.count_ref, bf16[256,512]{1,0:T(8,128)(2,1)} %bitcast.12, bf16[6,128,128]{2,1,0:T(8,128)(2,1)} %bitcast.13, s32[16,32]{1,0:T(8,128)} %bitcast.21, s32[1,16]{1,0:T(1,128)} %bitcast.23, ...), custom_call_target="tpu_custom_call" | custom-call | tf_op jit(solution)/shard_map/pallas_call | solution.py:349
  32.5 0.0 copy-start
  32.5 1.6 %copy.20 = bf16[1,128,512]{2,1,0:T(8,128)(2,1)} copy(bf16[1,128,512]{2,1,0:T(8,128)(2,1)} %bitcast.15) | data formatting | bytes 262144
  34.1 0.0 copy-done
  34.1 0.6 %copy.21 = f32[1,16,512]{2,1,0:T(8,128)} copy(f32[1,16,512]{2,1,0:T(8,128)S(1)} %bitcast.20) | data formatting | bytes 65536
Async XLA Ops:
  32.5 1.6 %copy-start = (f32[16,512]{1,0:T(8,128)S(1)}, f32[16,512]{1,0:T(8,128)}, u32[]{:S(2)}) copy-start(f32[16,512]{1,0:T(8,128)} %get-tuple-element.5) | copy-start | bytes 98308

commit v4 on v3

--- a/solution.py
+++ b/solution.py
@@ -34,8 +34,8 @@
 def kernel(
     n,
     lo,
-    cols_ref,
-    count_ref,
+    cols_hbm,
+    count_hbm,
     *refs,
 ):
     (
@@ -44,7 +44,7 @@
         out_x, out_w,
         feat, tiles, brows, bcount, cot, state, um, rm, ci, ch, ub, rb, cb,
         in_sem,
-        picks, adj, ext, halo_out, cot_all, wt_mine, wt, agg, gm_out, gm_in,
+        cols_ref, count_ref, scalar_sem, picks, adj, ext, halo_out, cot_all, wt_mine, wt, agg, gm_out, gm_in,
         ret_out, ret_in, gw_out, gw1_in, gw_mid, gw2_in, gws_out, gws_in, fin_out, fin_in,
         pair_send, pair_recv, halo_send, halo_recv, w1_send, w2_send, w_recv,
         ret_send, ret_recv, gw1_send, gw1_recv, gw2_send, gw2_recv,
@@ -68,6 +68,12 @@
     loads = [pltpu.make_async_copy(x, y, in_sem.at[i]) for i, (x, y) in enumerate(zip(hbm, vmem))]
     for load in loads:
         load.start()
+    scalars = (
+        pltpu.make_async_copy(cols_hbm, cols_ref, scalar_sem.at[0]),
+        pltpu.make_async_copy(count_hbm, count_ref, scalar_sem.at[1]),
+    )
+    for load in scalars:
+        load.start()
 
     def cols(which):
         return pl.ds(pl.multiple_of(which * half, half), half)
@@ -114,7 +120,7 @@
     picks[...] = (lax.broadcasted_iota(jnp.int32, (nodes, n * nb), 0) == rowsel).astype(F32).astype(BF16)
     halo_out[...] = dot(picks[...], feat[:, mine_cols], TN).astype(BF16)
 
-    for load in loads[3:5]:
+    for load in loads[3:5] + list(scalars):
         load.wait()
     for c in range(ncb):
         index = jnp.int32(0)
@@ -256,9 +262,23 @@
 
     gm_copy.wait()
     grad_summed = ((mixed_mine + gm_in[...].astype(F32)) / degree).astype(BF16)
-    ret_out[...] = dot(adj[:, nodes:], grad_summed, TN).astype(BF16)
     ret = (ret_out, ret_in, ret_send, ret_recv)
-    spread_start(*ret)
+    per_tile = TILE // nb
+    tiles_all = n // per_tile
+
+    def send_tile(t):
+        tile_no = lax.rem(me // per_tile + 1 + t, tiles_all)
+        piece = dot(adj[:, pl.ds(pl.multiple_of(nodes + tile_no * TILE, TILE), TILE)], grad_summed, TN)
+        ret_out[at(tile_no, TILE), :] = piece.astype(BF16)
+        for i in range(per_tile):
+            q = tile_no * per_tile + lax.rem(me + i, per_tile)
+
+            @pl.when(q != me)
+            def _():
+                spread_copy(lax.rem(q - me + n, n), *ret).start()
+
+    for t in range(tiles_all):
+        send_tile(t)
     ret_in[at(me, nb), :] = ret_out[at(me, nb), :]
     grad_local = dot(adj[:, :nodes], grad_summed, TN)
 
@@ -303,6 +323,17 @@
         gw2_copy(dz).wait_send()
     spread_drain(*halo)
     spread_drain(*ret)
+
+
+def store(x_ref, w_ref, x_out, w_out, sem):
+    copies = (
+        pltpu.make_async_copy(x_ref, x_out, sem.at[0]),
+        pltpu.make_async_copy(w_ref, w_out, sem.at[1]),
+    )
+    for copy in copies:
+        copy.start()
+    for copy in copies:
+        copy.wait()
 
 
 def local(
@@ -344,7 +375,6 @@
     arrays = arrays + maps + biases
     hbm = pl.BlockSpec(memory_space=pltpu.HBM)
     vmem = pl.BlockSpec(memory_space=pltpu.VMEM)
-    smem = pl.BlockSpec(memory_space=pltpu.SMEM)
     dma = pltpu.SemaphoreType.DMA
     out_x, out_w = pl.pallas_call(
         functools.partial(kernel, n, lo),
@@ -352,11 +382,14 @@
             jax.ShapeDtypeStruct((TILE, width), BF16),
             jax.ShapeDtypeStruct((wrows // 2, width), F32),
         ),
-        in_specs=[smem, smem] + [hbm] * len(arrays),
+        in_specs=[hbm] * (len(arrays) + 2),
         out_specs=(vmem, vmem),
         scratch_shapes=[pltpu.VMEM(x.shape, x.dtype) for x in arrays]
         + [
             dma((len(arrays),)),
+            pltpu.SMEM((1, tile_cols.shape[2]), jnp.int32),
+            pltpu.SMEM((1, 1), jnp.int32),
+            dma((2,)),
             pltpu.VMEM((nodes, n * nb), BF16),
             pltpu.VMEM((nodes, ncb * TILE), BF16),
             pltpu.VMEM((ncb * TILE, half), BF16),
@@ -395,6 +428,16 @@
             collective_id=0, has_side_effects=True, vmem_limit_bytes=60 << 20
         ),
     )(tile_cols[0], tile_count, *arrays)
+    out_x, out_w = pl.pallas_call(
+        store,
+        out_shape=(
+            jax.ShapeDtypeStruct(out_x.shape, BF16),
+            jax.ShapeDtypeStruct(out_w.shape, F32),
+        ),
+        in_specs=[vmem, vmem],
+        out_specs=(hbm, hbm),
+        scratch_shapes=[dma((2,))],
+    )(out_x, out_w)
     return out_x[None], out_w[None]
 
 

time: 34.9 us -> 33.5 us (0.960)
  local copies, waits for them, and re-layouts: 2.19 us -> 0 us
  Pallas kernels: 31.3 us -> 32 us
    unnamed x4 -> x0, local copies, waits for them, and re-layouts: 2.19 us -> none
    pallas_call x0 -> x1, Pallas kernels: none -> 1.58 us  [local(): pl.pallas_call(store, out_shape=(jax.ShapeDtypeStruct(out_x.shape, BF16),...]
    pallas_call x1, Pallas kernels: 31.3 us -> 30.5 us  [local(): pl.pallas_call(functools.partial(kernel, n, lo), out_shape=(jax.ShapeDtyp...]
where the time goes in v4:
time: 33.5 us; the launch traced here: 33.3 us
  Pallas kernels  32 us (96%)
  between operations  1.29 us (4%)
    pallas_call x1, Pallas kernels, local(): pl.pallas_call(functools.partial(kernel, n, lo), out_shape=(jax.ShapeDtyp...  30.5 us
    pallas_call x1, Pallas kernels, local(): pl.pallas_call(store, out_shape=(jax.ShapeDtypeStruct(out_x.shape, BF16),...  1.58 us

profile of v4, /device:TPU:0, one launch (start us, length us, event | category | flops | bytes accessed | tf_op | source)
XLA Modules:
  0.0 33.3 jit_solution(9626516043857038807)
XLA Ops:
  1.3 30.5 %shard_map.158 = (bf16[128,512]{1,0:T(8,128)(2,1)}, f32[16,512]{1,0:T(8,128)}) custom-call(s32[1,6]{1,0:T(1,128)} %bitcast.20, s32[1,1]{1,0:T(1,128)S(6)} %copy.17.count_hbm, bf16[256,512]{1,0:T(8,128)(2,1)} %bitcast.12, bf16[6,128,128]{2,1,0:T(8,128)(2,1)} %bitcast.13, s32[16,32]{1,0:T(8,128)} %bitcast.19, s32[1,16]{1,0:T(1,128)} %bitcast.21, ...), custom_call_target="tpu_custom_call" | custom-call | tf_op jit(solution)/shard_map/pallas_call | solution.py:379
  31.8 1.6 %shard_map.159 = (bf16[128,512]{1,0:T(8,128)(2,1)}, f32[16,512]{1,0:T(8,128)}) custom-call(bf16[128,512]{1,0:T(8,128)(2,1)} %get-tuple-element.6.x_ref, f32[16,512]{1,0:T(8,128)} %get-tuple-element.7.w_ref), custom_call_target="tpu_custom_call" | custom-call | tf_op jit(solution)/shard_map/pallas_call | solution.py:431
